TPU v7x, 512 devices: a whole 4x8x8 slice. The times are simulated.
512 devices in a mesh: src: 16 (over x, y_hi), snk: 32 (over z, y_lo, core).
Axes of the slice: x: 4, y: 8 (y_hi: 4, y_lo: 2; y = y_hi * 2 + y_lo), z: 8, core: 2. Of those that a mesh axis runs over, the one named last changes fastest.
Arguments:
- perambulator: bfloat16 [128, 32, 256, 512], P('snk', 'src'), may hold values from -0.25 to 0.25
- sink_elemental: bfloat16 [128, 256, 512], P('snk', 'src'), may hold values from -0.25 to 0.25
- source_elemental: bfloat16 [32, 256, 512], P('src', 'snk'), may hold values from -0.25 to 0.25
Outputs:
- correlator: float32 [4, 32, 128], P(None, 'src', 'snk')
All inputs are finite; a program needn't handle non-finite values.
Results may differ from a plain program's by a relative error of at most 0.0065.
Values may be sent and summed in bfloat16 or wider, within the bound.
A program may use at most 64 MiB of HBM per device.

v0:
```python
import jax
import jax.numpy as jnp
from jax import lax
from jax.sharding import PartitionSpec as P

DT = 1


def passed_along(value, axis, steps):
    count = lax.axis_size(axis)
    pairs = [(source, (source + steps) % count) for source in range(count)]
    return lax.ppermute(value, axis, pairs)


def complex_product(factor, second):
    order = second.shape[0]
    lower = jnp.concatenate([-second[:, order:], second[:, :order]], 1)
    stacked = jnp.concatenate([second, lower], 0)
    return jnp.dot(factor, stacked, preferred_element_type=jnp.float32)


def adjoint(matrix):
    order = matrix.shape[0]
    return jnp.concatenate([matrix[:, :order].T, -matrix[:, order:].T], 1)


def trace_adjoint(first, second):
    order = first.shape[0]
    first = first.astype(jnp.float32)
    second = second.astype(jnp.float32)
    real_part = jnp.sum(first[:, :order] * second[:, :order] + first[:, order:] * second[:, order:])
    imag_part = jnp.sum(first[:, order:] * second[:, :order] - first[:, :order] * second[:, order:])
    return (real_part, imag_part)


def make_first(sink_elem, tau_now, source_elem):
    head = complex_product(sink_elem, tau_now).astype(jnp.bfloat16)
    return complex_product(head, source_elem).astype(jnp.bfloat16)


def make_other(sink_elem, tau_now, source_elem):
    back = complex_product(adjoint(sink_elem), tau_now).astype(jnp.bfloat16)
    return complex_product(back, adjoint(source_elem)).astype(jnp.bfloat16)


def contract(first, tau_now, tau_next, other_next):
    swapped = complex_product(first, adjoint(tau_next)).astype(jnp.bfloat16)
    loop_product = complex_product(swapped, other_next)
    box_re, box_im = trace_adjoint(loop_product, tau_now)
    one_re, one_im = trace_adjoint(first, tau_now)
    two_re, two_im = trace_adjoint(other_next, tau_next)
    return jnp.stack(
        [one_re * two_re - one_im * two_im, one_re * two_im + one_im * two_re, box_re, box_im]
    )


def over_grid(func):
    return jax.vmap(jax.vmap(func, in_axes=(None, 0, 0)), in_axes=(0, 0, None))


def shards(perambulator, sink_elemental, source_elemental):
    sink_full = lax.all_gather(sink_elemental, "src", axis=1, tiled=True)
    source_full = lax.all_gather(source_elemental, "snk", axis=1, tiled=True)
    firsts = over_grid(make_first)(sink_full, perambulator, source_full)
    others = over_grid(make_other)(sink_full, perambulator, source_full)
    tau_edge, other_edge = passed_along((perambulator[:DT], others[:DT]), "snk", -1)
    tau_shifted = jnp.concatenate([perambulator[DT:], tau_edge], 0)
    other_shifted = jnp.concatenate([others[DT:], other_edge], 0)
    values = jax.vmap(jax.vmap(contract))(firsts, perambulator, tau_shifted, other_shifted)
    return jnp.transpose(values, (2, 1, 0))


def solution(mesh):
    in_specs = (P("snk", "src", None, None), P("snk", "src", None), P("src", "snk", None))
    out_specs = P(None, "src", "snk")
    return jax.shard_map(shards, mesh=mesh, in_specs=in_specs, out_specs=out_specs, check_vma=False)
```

profile of v0, /device:TPU:4, one launch (start us, length us, event | category | flops | bytes accessed | tf_op | source)
XLA Modules:
  0.0 116.5 jit_solution(15390691020452092340)
XLA Ops:
  6.5 0.0 all-gather.2.cloned.1.call-start
  6.5 0.7 all-gather.2.cloned.1.call-update
  7.3 0.0 copy-start
  7.3 1.2 %slice.126 = bf16[1,2,256,512]{3,2,1,0:T(8,128)(2,1)S(1)} slice(bf16[4,2,256,512]{3,2,1,0:T(8,128)(2,1)} %param.3), slice={[0:1], [0:2], [0:256], [0:512]} | slice | bytes 1048576 | tf_op jit(solution)/shard_map/slice | solution.py:66
  8.5 11.4 %collective-permute-start.1 = (bf16[1,2,256,512]{3,2,0,1:T(8,128)(2,1)S(1)}, bf16[1,2,256,512]{3,2,0,1:T(8,128)(2,1)S(1)}, u32[]{:S(2)}, u32[]{:S(2)}) collective-permute-start(bf16[1,2,256,512]{3,2,0,1:T(8,128)(2,1)S(1)} %copy.45), channel_id=1, source_target_pairs={{0,31},{1,0},{2,1},{3,2},{4,3},{5,4},{6,5},{7,6},{8,7},{9,8},{10,9... | collective-permute-start | bytes 1572872 | tf_op jit(solution)/shard_map/ppermute | solution.py:12
  20.0 38.2 %all_gather.7 = bf16[2,256,512]{2,1,0:T(8,128)(2,1)S(1)} all-gather(bf16[2,8,512]{2,1,0:T(8,128)(2,1)S(1)} %copy-done.6), channel_id=1, replica_groups=mesh['src'=16,'snk'=32] {'snk'}, dimensions={1}, use_global_device_ids=true | all-gather | bytes 540672 | tf_op jit(solution)/shard_map/all_gather | solution.py:63
  58.2 1.0 slice_bitcast_fusion.1
  59.2 1.5 %slice_negate_fusion = (bf16[4,2,256,256]{3,2,1,0:T(8,128)(2,1)}, bf16[4,2,256,256]{3,2,1,0:T(8,128)(2,1)}) fusion(bf16[4,2,256,512]{3,2,1,0:T(8,128)(2,1)S(1)} %copy-done), kind=kLoop, calls=%fused_computation.67 | loop fusion | flops 524288 | bytes 4194304 | tf_op jit(solution)/shard_map/vmap(vmap())/neg | solution.py:17
  60.7 2.5 %copy_convert_fusion = f32[4,2,256,512]{3,2,0,1:T(8,128)} fusion(bf16[4,2,256,512]{3,2,1,0:T(8,128)(2,1)S(1)} %copy-done), kind=kLoop, calls=%fused_computation.81 | loop fusion | flops 1048576 | bytes 6291456 | tf_op jit(solution)/shard_map/vmap(vmap())/convert_element_type | solution.py:30
  63.2 0.0 collective-permute-done.1
  63.2 1.1 fusion.41
  64.3 1.7 %fusion.69 = (bf16[4,2,256,256]{2,3,0,1:T(8,128)(2,1)}, bf16[4,2,256,256]{2,3,0,1:T(8,128)(2,1)}) fusion(bf16[1,2,256,512]{3,2,0,1:T(8,128)(2,1)S(1)} %collective-permute-done.1, bf16[4,2,256,512]{3,2,1,0:T(8,128)(2,1)S(1)} %copy-done), kind=kLoop, calls=%fused_computation.82 | loop fusion | flops 3670016 | bytes 4194304 | tf_op jit(solution)/shard_map/vmap(vmap())/neg | solution.py:24
  66.0 2.5 %fusion.14 = f32[4,2,256,512]{3,2,0,1:T(8,128)} fusion(bf16[1,2,256,512]{3,2,0,1:T(8,128)(2,1)S(1)} %collective-permute-done.1, bf16[4,2,256,512]{3,2,1,0:T(8,128)(2,1)S(1)} %copy-done), kind=kLoop, calls=%fused_computation.26 | loop fusion | flops 4194304 | bytes 6291456 | tf_op jit(solution)/shard_map/vmap(vmap())/convert_element_type | solution.py:30
  68.6 3.5 %all-gather.2.cloned.1.call-done = bf16[4,256,512]{2,1,0:T(8,128)(2,1)} async-done(((bf16[4,16,512]{2,1,0:T(8,128)(2,1)}), bf16[4,256,512]{2,1,0:T(8,128)(2,1)}) %all-gather.2.cloned.1.call-update) | async-done | bytes 1048592 | tf_op jit(solution)/shard_map/all_gather | solution.py:62
  72.1 2.1 %slice_bitcast_fusion = (bf16[4,256,256]{1,2,0:T(8,128)(2,1)S(1)}, bf16[4,256,256]{1,2,0:T(8,128)(2,1)}) fusion(bf16[4,256,512]{2,1,0:T(8,128)(2,1)} %all-gather.2.cloned.1.call-done), kind=kLoop, calls=%fused_computation.70 | loop fusion | flops 262144 | bytes 2097152 | tf_op jit(solution)/shard_map/vmap(vmap())/transpose | solution.py:24
  74.1 5.3 %convert_bitcast_fusion = bf16[4,2,256,512]{3,2,0,1:T(8,128)(2,1)} fusion(bf16[4,256,256]{1,2,0:T(8,128)(2,1)} %get-tuple-element.20, bf16[4,256,256]{1,2,0:T(8,128)(2,1)S(1)} %get-tuple-element.19, bf16[2,256,256]{1,2,0:T(8,128)(2,1)} %get-tuple-element.22, bf16[2,256,256]{1,2,0:T(8,128)(2,1)} %get-tuple-element.21, bf16[2,256,256]{1,2,0:T(8,128)(2,1)S(1)} %fusion.68, ...), kind=kOutput, calls=%fused_computation.37 | convolution fusion | flops 2168455168 | bytes 8126464 | tf_op jit(solution)/shard_map/vmap(vmap())/dot_general | solution.py:19
  79.5 2.8 %slice.122 = bf16[3,2,256,512]{3,2,0,1:T(8,128)(2,1)} slice(bf16[4,2,256,512]{3,2,0,1:T(8,128)(2,1)} %convert_bitcast_fusion), slice={[1:4], [0:2], [0:256], [0:512]} | slice | bytes 3145728 | tf_op jit(solution)/shard_map/slice | solution.py:68
  82.3 1.9 %slice.123 = bf16[1,2,256,512]{3,2,0,1:T(8,128)(2,1)} slice(bf16[4,2,256,512]{3,2,0,1:T(8,128)(2,1)} %convert_bitcast_fusion), slice={[0:1], [0:2], [0:256], [0:512]} | slice | bytes 1048576 | tf_op jit(solution)/shard_map/slice | solution.py:66
  84.1 5.4 %collective-permute-start = (bf16[1,2,256,512]{3,2,0,1:T(8,128)(2,1)}, bf16[1,2,256,512]{3,2,0,1:T(8,128)(2,1)S(1)}, u32[]{:S(2)}, u32[]{:S(2)}) collective-permute-start(bf16[1,2,256,512]{3,2,0,1:T(8,128)(2,1)} %slice.123), channel_id=1, source_target_pairs={{0,31},{1,0},{2,1},{3,2},{4,3},{5,4},{6,5},{7,6},{8,7},{9,8},{10,9... | collective-permute-start | bytes 1572872 | tf_op jit(solution)/shard_map/ppermute | solution.py:12
  89.6 0.0 copy-done.5
  89.6 5.6 %fusion.71 = (f32[4,2,256,512]{3,2,0,1:T(8,128)}, bf16[4,2,256,512]{3,2,0,1:T(8,128)(2,1)}) fusion(bf16[2,256,256]{2,1,0:T(8,128)(2,1)S(1)} %copy-done.5, bf16[2,256,256]{2,1,0:T(8,128)(2,1)} %get-tuple-element.24, bf16[2,256,512]{2,1,0:T(8,128)(2,1)S(1)} %all_gather.7, bf16[4,256,512]{2,1,0:T(8,128)(2,1)} %all-gather.2.cloned.1.call-done, ...), kind=kOutput, calls=%fused_computation.83 | convolution fusion | flops 2166358016 | bytes 12582912 | tf_op jit(solution)/shard_map/vmap(vmap())/dot_general | solution.py:19
  95.3 4.2 %fusion.27 = bf16[4,2,256,512]{3,2,1,0:T(8,128)(2,1)S(1)} fusion(bf16[4,2,256,512]{3,2,0,1:T(8,128)(2,1)} %get-tuple-element.28, bf16[4,2,256,256]{2,3,0,1:T(8,128)(2,1)} %fusion.41, bf16[4,2,256,256]{2,3,0,1:T(8,128)(2,1)} %get-tuple-element.14, bf16[4,2,256,256]{2,3,0,1:T(8,128)(2,1)} %get-tuple-element.13), kind=kOutput, calls=%fused_computation.43 | convolution fusion | flops 1091567616 | bytes 7340032 | tf_op jit(solution)/shard_map/vmap(vmap())/dot_general | solution.py:19
  99.5 0.0 collective-permute-done
  99.5 0.3 fusion.15
  99.8 1.9 %copy-done.1 = f32[4,2,256,512]{3,2,0,1:T(8,128)S(1)} copy-done((f32[4,2,256,512]{3,2,0,1:T(8,128)S(1)}, f32[4,2,256,512]{3,2,0,1:T(8,128)}, u32[]{:S(2)}) %copy-start.1) | copy-done | bytes 4194328
  101.6 0.9 subtract_reduce_fusion.1
  102.5 0.2 fusion.45
  102.8 1.5 %fusion = f32[4,2,256,512]{3,2,0,1:T(8,128)S(1)} fusion(bf16[4,2,256,256]{3,2,0,1:T(8,128)(2,1)S(1)} %get-tuple-element.16, bf16[4,2,256,256]{3,2,0,1:T(8,128)(2,1)S(1)} %get-tuple-element.15, bf16[1,2,256,512]{3,2,0,1:T(8,128)(2,1)S(1)} %collective-permute-done, bf16[3,2,256,512]{3,2,0,1:T(8,128)(2,1)S(1)} %copy-done.3, bf16[4,2,256,512]{3,2,1,0:T(8,128)(2,1)S(1)} %fusion.27), kind=kOutput, calls=%fused_computation.2 | convolution fusion | flops 1090519040 | bytes 10485760 | tf_op jit(solution)/shard_map/vmap(vmap())/dot_general | solution.py:19
  104.2 0.7 copy-done.2
  104.9 1.3 %copy-done.4 = f32[4,2,256,512]{3,2,0,1:T(8,128)S(1)} copy-done((f32[4,2,256,512]{3,2,0,1:T(8,128)S(1)}, f32[4,2,256,512]{3,2,0,1:T(8,128)}, u32[]{:S(2)}) %copy-start.4) | copy-done | bytes 4194328
  106.2 2.8 %add_reduce_fusion.2 = (f32[4,2]{0,1:T(2,128)S(1)}, f32[4,2]{0,1:T(2,128)S(1)}, f32[4,2]{0,1:T(2,128)S(1)}, f32[4,2]{0,1:T(2,128)S(1)}) fusion(f32[4,2,256,512]{3,2,0,1:T(8,128)S(1)} %copy-done.4, f32[4,2,256,512]{3,2,0,1:T(8,128)S(1)} %copy-done.2, f32[4,2,256,512]{3,2,0,1:T(8,128)S(1)} %fusion), kind=kLoop, calls=%fused_computation.40 | loop fusion | flops 8388576 | bytes 12583040 | tf_op jit(solution)/shard_map/vmap(vmap())/reduce_sum | solution.py:31
  109.0 0.6 maximum_bitcast_fusion.7
  (12 shorter events, 0.1 us)
Async XLA Ops:
  6.5 13.4 %copy-start.6 = (bf16[2,8,512]{2,1,0:T(8,128)(2,1)S(1)}, bf16[2,8,512]{2,1,0:T(8,128)(2,1)}, u32[]{:S(2)}) copy-start(bf16[2,8,512]{2,1,0:T(8,128)(2,1)} %param.5) | copy-start | bytes 49156
  6.5 65.5 %all-gather.2.cloned.1.call-start = ((), (), s32[]{:S(2)}) async-start(), calls=%async_computation | async-start | bytes 1114112 | tf_op jit(solution)/shard_map/all_gather | solution.py:62
  7.3 52.0 %copy-start = (bf16[4,2,256,512]{3,2,1,0:T(8,128)(2,1)S(1)}, bf16[4,2,256,512]{3,2,1,0:T(8,128)(2,1)}, u32[]{:S(2)}) copy-start(bf16[4,2,256,512]{3,2,1,0:T(8,128)(2,1)} %param.3) | copy-start | bytes 6291460
  8.5 54.7 %collective-permute-start.1 = (bf16[1,2,256,512]{3,2,0,1:T(8,128)(2,1)S(1)}, bf16[1,2,256,512]{3,2,0,1:T(8,128)(2,1)S(1)}, u32[]{:S(2)}, u32[]{:S(2)}) collective-permute-start(bf16[1,2,256,512]{3,2,0,1:T(8,128)(2,1)S(1)} %copy.45), channel_id=1, source_target_pairs={{0,31},{1,0},{2,1},{3,2},{4,3},{5,4},{6,5},{7,6},{8,7},{9,8},{10,9... | collective-permute-start | bytes 1572872 | tf_op jit(solution)/shard_map/ppermute | solution.py:12
  79.5 10.1 %copy-start.5 = (bf16[2,256,256]{2,1,0:T(8,128)(2,1)S(1)}, bf16[2,256,256]{2,1,0:T(8,128)(2,1)}, u32[]{:S(2)}) copy-start(bf16[2,256,256]{2,1,0:T(8,128)(2,1)} %get-tuple-element.23) | copy-start | bytes 786436
  84.1 15.3 %collective-permute-start = (bf16[1,2,256,512]{3,2,0,1:T(8,128)(2,1)}, bf16[1,2,256,512]{3,2,0,1:T(8,128)(2,1)S(1)}, u32[]{:S(2)}, u32[]{:S(2)}) collective-permute-start(bf16[1,2,256,512]{3,2,0,1:T(8,128)(2,1)} %slice.123), channel_id=1, source_target_pairs={{0,31},{1,0},{2,1},{3,2},{4,3},{5,4},{6,5},{7,6},{8,7},{9,8},{10,9... | collective-permute-start | bytes 1572872 | tf_op jit(solution)/shard_map/ppermute | solution.py:12
  95.2 4.2 %copy-start.3 = (bf16[3,2,256,512]{3,2,0,1:T(8,128)(2,1)S(1)}, bf16[3,2,256,512]{3,2,0,1:T(8,128)(2,1)}, u32[]{:S(2)}) copy-start(bf16[3,2,256,512]{3,2,0,1:T(8,128)(2,1)} %slice.122) | copy-start | bytes 4718596
  99.5 2.2 %copy-start.1 = (f32[4,2,256,512]{3,2,0,1:T(8,128)S(1)}, f32[4,2,256,512]{3,2,0,1:T(8,128)}, u32[]{:S(2)}) copy-start(f32[4,2,256,512]{3,2,0,1:T(8,128)} %fusion.14) | copy-start | bytes 12582916
  102.7 2.2 %copy-start.2 = (f32[4,2,256,512]{3,2,0,1:T(8,128)S(1)}, f32[4,2,256,512]{3,2,0,1:T(8,128)}, u32[]{:S(2)}) copy-start(f32[4,2,256,512]{3,2,0,1:T(8,128)} %copy_convert_fusion) | copy-start | bytes 12582916
  102.8 3.5 %copy-start.4 = (f32[4,2,256,512]{3,2,0,1:T(8,128)S(1)}, f32[4,2,256,512]{3,2,0,1:T(8,128)}, u32[]{:S(2)}) copy-start(f32[4,2,256,512]{3,2,0,1:T(8,128)} %get-tuple-element.27) | copy-start | bytes 12582916
Sparse Core Ops, SparseCore 0:
  10.4 61.5 all-gather.1
where the time goes:
time: 117 us; the launch traced here: 116 us
  blocking collectives  38.2 us (33%)
  other arithmetic  17.2 us (15%)
  starting transfers between devices  16.8 us (14%)
  matrix products  16.6 us (14%)
  between operations  13.5 us (12%)
  local copies, waits for them, and re-layouts  9.8 us (8%)
  waiting for transfers between devices  4.23 us (4%)
    all_gather x1, blocking collectives, shards(): source_full = lax.all_gather(source_elemental, 'snk', axis=1, tiled=True)  38.2 us
    ppermute x2, starting transfers between devices, passed_along(): return lax.ppermute(value, axis, pairs)  16.8 us
    dot_general x4, matrix products, complex_product(): return jnp.dot(factor, stacked, preferred_element_type=jnp.float32)  16.6 us
    convert_element_type x2, other arithmetic, trace_adjoint(): second = second.astype(jnp.float32)  5.07 us
    transpose x3, other arithmetic, adjoint(): return jnp.concatenate([matrix[:, :order].T, -matrix[:, order:].T], 1)  4.17 us
    unnamed x15, local copies, waits for them, and re-layouts  3.92 us
    all_gather x1, waiting for transfers between devices, shards(): sink_full = lax.all_gather(sink_elemental, 'src', axis=1, tiled=True)  3.51 us
    reduce_sum x1, other arithmetic, trace_adjoint(): jnp.sum(first[:, :order] * second[:, :order] + first[:, order:] * second[...  2.82 us
  transfers between devices with their start and end apart: 3, of which 1 were waited for; matrix products, arithmetic and copies ran while one was open for 18% of the time, Pallas kernels for 0%

commit v1 on v0

v1 whole, which is shorter than its diff:
```python
import jax
import jax.numpy as jnp
from jax import lax
from jax.experimental import pallas as pl
from jax.experimental.pallas import tpu as pltpu
from jax.sharding import PartitionSpec as P

NX, NYH, NZ = 4, 4, 8
T, S, N = 4, 2, 256
W = 2 * N
ROWS = 16
BF, F32 = jnp.bfloat16, jnp.float32


def mm(a, b):
    return lax.dot_general(a, b, (((1,), (0,)), ((), ())), preferred_element_type=F32)


def mm_nt(a, b):
    return lax.dot_general(a, b, (((1,), (1,)), ((), ())), preferred_element_type=F32)


def trace_adjoint(pr, pi, qr, qi):
    pr, pi, qr, qi = (v.astype(F32) for v in (pr, pi, qr, qi))
    return jnp.sum(pr * qr + pi * qi), jnp.sum(pi * qr - pr * qi)


def halves(m):
    return m[:, :N], m[:, N:]


def upright(m):
    return jnp.concatenate([m[:, :N], m[:, N:]], axis=0)


def lower_rows(m):
    return jnp.concatenate([-m[:, N:], m[:, :N]], axis=1)


def kernel(
    tau, sink, slab, out,
    tbig, tadj, tlast, abuf, bslab, edge, gbuf, bbig, bleft, badj, ubig, vbig, dre, dim,
    tau_sem, own_sem, y_send, y_recv, x_send, x_recv, f_send, f_recv,
    l_send, l_recv, z_send, z_recv, c_send, c_recv, e_send, e_recv,
):
    j, k = lax.axis_index("src"), lax.axis_index("snk")
    x, yh = j // NYH, j % NYH
    c, q = k % 2, k // 2
    yl, z = q % 2, q // 2

    def at(xx, yy):
        return (lax.rem(xx + NX, NX) * NYH + lax.rem(yy + NYH, NYH), k)

    def along_z(d):
        return (j, lax.rem(z + d, NZ) * 4 + yl * 2 + c)

    before = (j, lax.rem(k + 4 * NZ - 1, 4 * NZ))
    after = (j, lax.rem(k + 1, 4 * NZ))
    other_core = (j, k + 1 - 2 * c)
    other_y = (j, k + 2 - 4 * yl)

    def remote(src, dst, send, recv, device):
        return pltpu.make_async_remote_copy(
            src_ref=src, dst_ref=dst, send_sem=send, recv_sem=recv,
            device_id=device, device_id_type=pl.DeviceIdType.MESH,
        )

    loads = {}
    for t in range(T):
        for s in range(S):
            into = tbig.at[t, s, pl.ds(0, N)] if t < T - 1 else tlast.at[s]
            loads[t, s] = pltpu.make_async_copy(tau.at[t, s], into, tau_sem.at[t, s])
            loads[t, s].start()
    mine = pl.ds(pl.multiple_of(64 * x + ROWS * yh, ROWS), ROWS)
    owns = [pltpu.make_async_copy(sink.at[t], abuf.at[t, mine], own_sem.at[t]) for t in range(T)]
    owns.append(pltpu.make_async_copy(slab, bslab.at[c, q], own_sem.at[T]))
    for copy in owns:
        copy.start()

    barrier = pltpu.get_barrier_semaphore()
    peers = [at(x, yh + d) for d in range(1, NYH)] + [at(x + 1, yh), at(x - 1, yh)]
    peers += [before, after, other_y] + [along_z(d) for d in range(1, NZ)]
    for peer in peers:
        pl.semaphore_signal(barrier, inc=1, device_id=peer, device_id_type=pl.DeviceIdType.MESH)
    pl.semaphore_wait(barrier, len(peers))

    ys, xs, fs = {}, {}, {}
    started = []

    def go(copy):
        copy.start()
        started.append(copy)
        return copy

    ylo = go(remote(slab, bslab.at[c, q], l_send, l_recv, other_y))
    for t in range(T):
        for d in range(1, NYH):
            ys[t, d] = go(remote(
                sink.at[t], abuf.at[t, mine], y_send.at[t, d - 1], y_recv.at[t, d - 1], at(x, yh + d)
            ))

    def block(xx, start=0, size=64):
        first = pl.multiple_of(64 * lax.rem(xx + NX, NX) + start, 32)
        return pl.ds(first, size)

    def to_x(t):
        owns[t].wait()
        for d in range(1, NYH):
            ys[t, d].wait_recv()
        for way, step in ((0, 1), (1, -1)):
            rows = abuf.at[t, block(x)]
            xs[t, way] = go(remote(rows, rows, x_send.at[t, way], x_recv.at[t, way], at(x + step, yh)))

    def forward(t):
        for way, step in ((0, 1), (1, -1)):
            xs[t, way].wait_recv()
            rows = abuf.at[t, block(x - step, 32 * way, 32)]
            fs[t, way] = go(remote(rows, rows, f_send.at[t, way], f_recv.at[t, way], at(x + step, yh)))

    def arrived(t):
        for way in range(2):
            fs[t, way].wait_recv()

    def per_source(body):
        lax.fori_loop(0, S, lambda s, carry: (body(s), carry)[1], 0)

    def prepare(t):
        for s in range(S):
            loads[t, s].wait()

        def body(s):
            m = tbig[t, s, :N]
            tbig[t, s, N:] = lower_rows(m)
            re, im = m[:, :N].T, m[:, N:].T
            tadj[t, s, :N, :N] = re
            tadj[t, s, :N, N:] = im
            tadj[t, s, N:, :N] = -im
            tadj[t, s, N:, N:] = re

        per_source(body)

    def sandwich(t):
        def body(s):
            head = mm(abuf[t], tbig[t, s]).astype(BF)
            g = mm(tadj[t, s], upright(head)).astype(BF)
            gbuf[t, s, :, :N] = g[:N]
            gbuf[t, s, :, N:] = g[N:]

        per_source(body)

    def one_trace(t, g, s):
        dre[t, s], dim[t, s] = trace_adjoint(*halves(g), *halves(badj[s]))

    def box_of(t):
        def body(s):
            left = mm(gbuf[t, s], bbig[s])
            right = mm(bleft[s], upright(gbuf[t + 1, s]))
            out[2, s, t], out[3, s, t] = trace_adjoint(*halves(left), right[:N], right[N:])

        per_source(body)

    prepare(0)
    to_x(0)
    ylo.wait_recv()
    owns[T].wait()
    zs = []
    two = bslab.at[c, pl.ds(2 * z, 2)]
    for d in range(1, NZ):
        zs.append(go(remote(two, two, z_send.at[d - 1], z_recv.at[d - 1], along_z(d))))
    prepare(1)
    to_x(1)
    forward(0)
    prepare(2)
    to_x(2)
    forward(1)
    arrived(0)
    sandwich(0)
    edges = [go(remote(gbuf.at[0, s], edge.at[s], e_send.at[s], e_recv.at[s], before)) for s in range(S)]
    to_x(3)
    forward(2)
    for copy in zs:
        copy.wait_recv()
    over = go(remote(bslab.at[c], bslab.at[c], c_send, c_recv, other_core))
    arrived(1)
    sandwich(1)
    forward(3)
    over.wait_recv()

    def spread(s):
        for n in range(16):
            first = bslab[0, n].astype(F32)
            second = bslab[1, n].astype(F32)
            low = jnp.where(s == 0, first[:8], first[8:])
            high = jnp.where(s == 0, second[:8], second[8:])
            bbig[s, pl.ds(ROWS * n, ROWS)] = jnp.concatenate([low, high], axis=0).astype(BF)
        m = bbig[s, :N]
        re, im = halves(m)
        bbig[s, N:] = lower_rows(m)
        bleft[s, :N, :N] = re
        bleft[s, :N, N:] = -im
        bleft[s, N:, :N] = im
        bleft[s, N:, N:] = re
        badj[s, :, :N] = re.T
        badj[s, :, N:] = -im.T

    per_source(spread)

    def outer(s):
        u = mm(tlast[s], bbig[s]).astype(BF)
        ubig[s, :N] = u
        ubig[s, N:] = lower_rows(u)
        v = mm_nt(tlast[s], bbig[s]).astype(BF)
        vbig[s, :N] = v
        vbig[s, N:] = lower_rows(v)

    for s in range(S):
        loads[T - 1, s].wait()
    per_source(outer)
    box_of(0)
    arrived(2)
    sandwich(2)
    box_of(1)

    def traces(s):
        for t in range(T - 1):
            one_trace(t, gbuf[t, s], s)

    per_source(traces)
    arrived(3)

    def last(s):
        a = halves(abuf[T - 1])
        dre[T - 1, s], dim[T - 1, s] = trace_adjoint(*a, *halves(mm_nt(tlast[s], ubig[s])))
        g = gbuf[T - 2, s]
        n = (mm(vbig[s, :N], jnp.concatenate([g, lower_rows(g)], axis=0))).astype(BF)
        out[2, s, T - 2], out[3, s, T - 2] = trace_adjoint(*halves(mm_nt(n, vbig[s])), *a)

    per_source(last)

    for copy in edges:
        copy.wait_recv()

    def final(s):
        a = halves(abuf[T - 1])
        g = edge[s]
        one_trace(T, g, s)
        n = mm(ubig[s, :N], jnp.concatenate([g, lower_rows(g)], axis=0)).astype(BF)
        out[2, s, T - 1], out[3, s, T - 1] = trace_adjoint(*a, *halves(mm_nt(n, ubig[s])))

    per_source(final)
    for s in range(S):
        for t in range(T):
            ar, ai, br, bi = dre[t, s], dim[t, s], dre[t + 1, s], dim[t + 1, s]
            out[0, s, t] = ar * br + ai * bi
            out[1, s, t] = ai * br - ar * bi
    for copy in started:
        copy.wait_send()


def shards(perambulator, sink_elemental, source_elemental):
    dma = pltpu.SemaphoreType.DMA
    vmem = pltpu.VMEM
    return pl.pallas_call(
        kernel,
        out_shape=jax.ShapeDtypeStruct((4, S, T), F32),
        in_specs=[pl.BlockSpec(memory_space=pl.ANY)] * 3,
        out_specs=pl.BlockSpec(memory_space=pltpu.SMEM),
        scratch_shapes=[
            vmem((T - 1, S, W, W), BF),
            vmem((T - 1, S, W, W), BF),
            vmem((S, N, W), BF),
            vmem((T, N, W), BF),
            vmem((2, 16, ROWS, W), BF),
            vmem((S, N, W), BF),
            vmem((T - 1, S, N, W), BF),
            vmem((S, W, W), BF),
            vmem((S, W, W), BF),
            vmem((S, N, W), BF),
            vmem((S, W, W), BF),
            vmem((S, W, W), BF),
            pltpu.SMEM((T + 1, S), F32),
            pltpu.SMEM((T + 1, S), F32),
            dma((T, S)),
            dma((T + 1,)),
            dma((T, NYH - 1)),
            dma((T, NYH - 1)),
            dma((T, 2)),
            dma((T, 2)),
            dma((T, 2)),
            dma((T, 2)),
            dma,
            dma,
            dma((NZ - 1,)),
            dma((NZ - 1,)),
            dma,
            dma,
            dma((S,)),
            dma((S,)),
        ],
        compiler_params=pltpu.CompilerParams(
            collective_id=0, has_side_effects=True, vmem_limit_bytes=48 * 1024 * 1024
        ),
        cost_estimate=pl.CostEstimate(flops=4_600_000_000, bytes_accessed=2_300_000, transcendentals=0),
    )(perambulator, sink_elemental, source_elemental.reshape(ROWS, W))


def solution(mesh):
    in_specs = (P("snk", "src", None, None), P("snk", "src", None), P("src", "snk", None))
    out_specs = P(None, "src", "snk")
    return jax.shard_map(shards, mesh=mesh, in_specs=in_specs, out_specs=out_specs, check_vma=False)
```

time: 117 us -> 46.9 us (0.40)
  the two profiles are of different devices: /device:TPU:4 before, /device:TPU:64 now
where the time goes in v1:
time: 46.9 us; the launch traced here: 46.6 us
  Pallas kernels  42.9 us (91%)
  local copies, waits for them, and re-layouts  3.74 us (8%)
    pallas_call x1, Pallas kernels, shards(): pl.pallas_call(kernel, out_shape=jax.ShapeDtypeStruct((4, S, T), F32), in...  42.9 us
    unnamed x7, local copies, waits for them, and re-layouts  3.74 us

profile of v1, /device:TPU:64, one launch (start us, length us, event | category | flops | bytes accessed | tf_op | source)
XLA Modules:
  0.0 46.6 jit_solution(3882671055876677384)
XLA Ops:
  0.0 0.0 copy-start
  0.0 1.6 %copy-done = bf16[4,2,256,512]{3,2,1,0:T(8,128)(2,1)S(1)} copy-done((bf16[4,2,256,512]{3,2,1,0:T(8,128)(2,1)S(1)}, bf16[4,2,256,512]{3,2,1,0:T(8,128)(2,1)}, u32[]{:S(2)}) %copy-start) | copy-done | bytes 2097176
  1.6 0.0 copy-start.1
  1.6 0.8 %copy-done.1 = bf16[4,16,512]{2,1,0:T(8,128)(2,1)S(1)} copy-done((bf16[4,16,512]{2,1,0:T(8,128)(2,1)S(1)}, bf16[4,16,512]{2,1,0:T(8,128)(2,1)}, u32[]{:S(2)}) %copy-start.1) | copy-done | bytes 65560
  2.4 0.0 copy-start.2
  2.4 0.7 %copy-done.2 = bf16[2,8,512]{2,1,0:T(8,128)(2,1)S(1)} copy-done((bf16[2,8,512]{2,1,0:T(8,128)(2,1)S(1)}, bf16[2,8,512]{2,1,0:T(8,128)(2,1)}, u32[]{:S(2)}) %copy-start.2) | copy-done | bytes 16408
  3.1 42.9 %shard_map.37 = f32[4,2,4]{2,1,0:T(2,128)S(1)} custom-call(bf16[4,2,256,512]{3,2,1,0:T(8,128)(2,1)S(1)} %copy-done, bf16[4,16,512]{2,1,0:T(8,128)(2,1)S(1)} %copy-done.1, bf16[16,512]{1,0:T(8,128)(2,1)S(1)} %bitcast.1), custom_call_target="tpu_custom_call" | custom-call | flops 4600000000 | bytes 2300000 | tf_op jit(solution)/shard_map/pallas_call | solution.py:263
  46.0 0.6 %copy.5 = f32[4,2,4]{2,1,0:T(2,128)} copy(f32[4,2,4]{2,1,0:T(2,128)S(1)} %shard_map.37) | data formatting | bytes 256
Async XLA Ops:
  0.0 1.6 %copy-start = (bf16[4,2,256,512]{3,2,1,0:T(8,128)(2,1)S(1)}, bf16[4,2,256,512]{3,2,1,0:T(8,128)(2,1)}, u32[]{:S(2)}) copy-start(bf16[4,2,256,512]{3,2,1,0:T(8,128)(2,1)} %tau.1) | copy-start | bytes 6291460
  1.6 0.8 %copy-start.1 = (bf16[4,16,512]{2,1,0:T(8,128)(2,1)S(1)}, bf16[4,16,512]{2,1,0:T(8,128)(2,1)}, u32[]{:S(2)}) copy-start(bf16[4,16,512]{2,1,0:T(8,128)(2,1)} %sink.1) | copy-start | bytes 196612
  2.4 0.7 %copy-start.2 = (bf16[2,8,512]{2,1,0:T(8,128)(2,1)S(1)}, bf16[2,8,512]{2,1,0:T(8,128)(2,1)}, u32[]{:S(2)}) copy-start(bf16[2,8,512]{2,1,0:T(8,128)(2,1)} %param.5) | copy-start | bytes 49156

commit v2 on v0

v2 whole, which is shorter than its diff:
```python
import jax
import jax.numpy as jnp
from jax import lax
from jax.experimental import pallas as pl
from jax.experimental.pallas import tpu as pltpu
from jax.sharding import PartitionSpec as P

NX, NYH, NZ = 4, 4, 8
STEP = (1, -1)
LAST = 4 * NZ - 1
T, S, N = 4, 2, 256
GROUPS = ((0, 2), (2, 2), (4, 1))
W = 2 * N
ROWS = 16
BF, F32 = jnp.bfloat16, jnp.float32


def mm(a, b):
    return lax.dot_general(a, b, (((1,), (0,)), ((), ())), preferred_element_type=F32)


def mm_nt(a, b):
    return lax.dot_general(a, b, (((1,), (1,)), ((), ())), preferred_element_type=F32)


def trace_adjoint(pr, pi, qr, qi):
    pr, pi, qr, qi = (v.astype(F32) for v in (pr, pi, qr, qi))
    return jnp.sum(pr * qr + pi * qi), jnp.sum(pi * qr - pr * qi)


def halves(m):
    return m[:, :N], m[:, N:]


def lower_rows(m):
    return jnp.concatenate([-m[:, N:], m[:, :N]], axis=1)


def kernel(
    tau, sink, slab, out,
    tall, abig, bslab, bbig, ubig, vdag, xbig, zlast, dout, dnext, dre, dim,
    tau_sem, own_sem, y_send, y_recv, v_send, v_recv, x_send, x_recv, f_send, f_recv,
    l_send, l_recv, z_send, z_recv, h_send, h_recv, e_send, e_recv, wrap_sem,
):
    j, k = lax.axis_index("src"), lax.axis_index("snk")
    x, yh = j // NYH, j % NYH
    c, q = k % 2, k // 2
    yl, z = q % 2, q // 2
    near = q + 1 - 2 * yl

    def at(xx, yy):
        return (lax.rem(xx + NX, NX) * NYH + lax.rem(yy + NYH, NYH), k)

    def along_z(d):
        return (j, lax.rem(z + d + NZ, NZ) * 4 + yl * 2 + c)

    before = (j, lax.rem(k + 4 * NZ - 1, 4 * NZ))
    after = (j, lax.rem(k + 1, 4 * NZ))
    other_core = (j, k + 1 - 2 * c)
    other_y = (j, k + 2 - 4 * yl)

    barrier = pltpu.get_barrier_semaphore()
    peers = [at(x, yh + 1), at(x, yh - 1), at(x + 1, yh), at(x - 1, yh)]
    peers += [other_y, other_core]

    def tell(semaphore, device):
        pl.semaphore_signal(semaphore, inc=1, device_id=device, device_id_type=pl.DeviceIdType.MESH)

    for peer in peers:
        tell(barrier, peer)

    @pl.when((c == 1) & (k < LAST))
    def _():
        tell(barrier, after)

    @pl.when(k == 0)
    def _():
        tell(barrier, before)

    for i in range(1, NZ):

        @pl.when(z + i < NZ)
        def _():
            tell(barrier, along_z(i))

    def chunk(xx, yy):
        row = 64 * lax.rem(xx + NX, NX) + ROWS * lax.rem(yy + NYH, NYH)
        return pl.ds(pl.multiple_of(row, ROWS), ROWS)

    mine = chunk(x, yh)
    own = pltpu.make_async_copy(sink, abig.at[pl.ds(0, T), mine], own_sem.at[0])
    own_slab = pltpu.make_async_copy(slab, bslab.at[c, q], own_sem.at[1])
    own.start()
    own_slab.start()
    loads = [
        pltpu.make_async_copy(tau.at[t, s], tall.at[s, t], tau_sem.at[t, s]) for t in range(T) for s in range(S)
    ]
    for copy in loads:
        copy.start()
    pl.semaphore_wait(barrier, len(peers) + z + (1 - c) * ((k + LAST) // (LAST + 1)) + (k + 1) // (LAST + 1))

    @pl.when(k == LAST)
    def _():
        tell(wrap_sem, after)

    def remote(src, dst, send, recv, device):
        return pltpu.make_async_remote_copy(
            src_ref=src, dst_ref=dst, send_sem=send, recv_sem=recv,
            device_id=device, device_id_type=pl.DeviceIdType.MESH,
        )

    def rows(g, xx, yy):
        return abig.at[pl.ds(*GROUPS[g]), chunk(xx, yy)]

    def first_rows(g):
        return sink.at[pl.ds(*GROUPS[g])] if g < 2 else rows(g, x, yh)

    def y_copy(g, way):
        device = at(x, yh + STEP[way])
        return remote(first_rows(g), rows(g, x, yh), y_send.at[g, way], y_recv.at[g, way], device)

    def v_copy(g):
        step = STEP[g % 2]
        far = rows(g, x, yh - step)
        return remote(far, far, v_send.at[g], v_recv.at[g], at(x, yh + step))

    def x_copy(g, d, way):
        src = first_rows(g) if d == 0 else rows(g, x, yh + d)
        device = at(x + STEP[way], yh)
        return remote(src, rows(g, x, yh + d), x_send.at[g, d, way], x_recv.at[g, d, way], device)

    def f_copy(g, d):
        step = STEP[d % 2]
        far = rows(g, x - step, yh + d)
        return remote(far, far, f_send.at[g, d], f_recv.at[g, d], at(x + step, yh))

    def guarded(func):
        def call(g, *rest):
            if g == 2:
                pl.when(c == 1)(lambda: func(g, *rest))
            else:
                func(g, *rest)

        return call

    @guarded
    def y_out(g):
        for way in range(2):
            y_copy(g, way).start()

    @guarded
    def x_out(g, d):
        for way in range(2):
            x_copy(g, d, way).start()

    @guarded
    def y_on(g):
        way = g % 2
        for w in (way, 1 - way):
            y_copy(g, w).wait_recv()
            if w == way:
                v_copy(g).start()
            for out_way in range(2):
                x_copy(g, (3, 1)[w], out_way).start()

    @guarded
    def y_end(g):
        v_copy(g).wait_recv()
        for way in range(2):
            x_copy(g, 2, way).start()

    @guarded
    def x_on(g, d):
        x_copy(g, d, d % 2).wait_recv()
        f_copy(g, d).start()

    @guarded
    def arrived(g):
        for d in range(NYH):
            x_copy(g, d, 1 - d % 2).wait_recv()
            f_copy(g, d).wait_recv()

    @guarded
    def all_sent(g):
        v_copy(g).wait_send()
        for way in range(2):
            y_copy(g, way).wait_send()
        for d in range(NYH):
            f_copy(g, d).wait_send()
            for way in range(2):
                x_copy(g, d, way).wait_send()

    def pair(zz):
        return bslab.at[c, pl.ds(2 * lax.rem(zz + NZ, NZ), 2)]

    def along(way, i):
        return z + i if way == 0 else z - i

    def inside(way, i):
        return z + i < NZ if way == 0 else z >= i

    def z_copy(way, i):
        return remote(
            pair(z), pair(z), z_send.at[1 - way, i - 1], z_recv.at[1 - way, i - 1], along_z(i if way == 0 else -i)
        )

    def z_wait(way, i):
        block = pair(along(way, i))
        return remote(block, block, z_send.at[way, i - 1], z_recv.at[way, i - 1], other_core)

    def hand(way, i):
        block = pair(along(way, i))
        return remote(block, block, h_send.at[way, i], h_recv.at[way, i], other_core)

    def down():
        for i in range(1, NZ):

            @pl.when(inside(1, i))
            def _():
                z_copy(1, i).start()

    def up(i):
        @pl.when(inside(0, i))
        def _():
            z_wait(0, i).wait_recv()
            z_copy(0, i).start()
            hand(0, i).start()

    def below(i):
        @pl.when(inside(1, i))
        def _():
            z_wait(1, i).wait_recv()
            hand(1, i).start()

    edges = [remote(tau.at[0, s], tall.at[s, T], e_send.at[s], e_recv.at[s], before) for s in range(S)]
    edge_a = remote(sink.at[0], abig.at[T, mine], e_send.at[S], e_recv.at[S], before)

    loc = remote(slab, bslab.at[c, q], l_send, l_recv, other_y)
    edge_whole = remote(abig.at[0, pl.ds(0, N)], abig.at[T, pl.ds(0, N)], e_send.at[S + 2], e_recv.at[S + 2], other_core)

    @guarded
    def next_rows(g):
        edge_a.wait_recv()
        y_out(g)
        x_out(g, 0)

    y_out(0)
    x_out(0, 0)
    loc.start()

    @pl.when((c == 0) & (k > 0))
    def _():
        edge_a.start()

    y_out(1)
    x_out(1, 0)
    own_slab.wait()
    loc.wait_recv()
    down()
    hand(0, 0).start()
    x_on(0, 0)
    y_on(0)
    next_rows(2)
    x_on(1, 0)
    y_on(1)

    @pl.when(k > 0)
    def _():
        for copy in edges:
            copy.start()

    up(1)
    y_end(0)
    x_on(0, 1)
    x_on(0, 3)
    up(2)
    y_on(2)
    y_end(1)
    up(3)
    x_on(1, 1)
    x_on(1, 3)
    up(4)
    x_on(2, 0)
    x_on(0, 2)
    y_end(2)
    up(5)
    x_on(1, 2)
    up(6)
    up(7)

    @pl.when(k == 0)
    def _():
        pl.semaphore_wait(wrap_sem, 1)
        edge_a.start()
        for copy in edges:
            copy.start()

    for i in range(1, NZ):
        below(i)
    x_on(2, 1)
    x_on(2, 3)
    hand(0, 0).wait_recv()
    for i in range(1, NZ):
        for way in range(2):

            @pl.when(inside(way, i))
            def _():
                hand(way, i).wait_recv()

    for s in range(S):
        for n in range(16):
            parts = [bslab[m, n].astype(F32)[8 * s : 8 * s + 8] for m in range(2)]
            bbig[s, ROWS * n : ROWS * (n + 1)] = jnp.concatenate(parts, axis=0).astype(BF)
        bbig[s, N:] = lower_rows(bbig[s, :N])
    for copy in loads:
        copy.wait()
    for s in range(S):
        u = mm(tall[s, :T].reshape(T * N, W), bbig[s]).astype(BF)
        for t in range(T):
            ubig[s, t, :N] = u[t * N : (t + 1) * N]
            ubig[s, t, N:] = lower_rows(u[t * N : (t + 1) * N])
        if s == 0:
            x_on(2, 2)

    def pairs(t):
        for s in range(S):
            both = mm_nt(tall[s, t : t + 2].reshape(2 * N, W), ubig[s, t])
            vdag[t, s] = both[:N]
            xd = both[N:].astype(BF)
            xbig[t, s, :N] = xd
            xbig[t, s, N:] = lower_rows(xd)

    def fill(t):
        abig[t, N:] = lower_rows(abig[t, :N])

    def trace_d(t):
        for s in range(S):
            dre[t, s], dim[t, s] = trace_adjoint(*halves(abig[t, :N]), *halves(vdag[t, s]))

    def right(t):
        return mm(xbig[t, :, :N].reshape(S * N, W), abig[t])

    def box(t, second):
        for s in range(S):
            first = mm(abig[t + 1, :N], xbig[t, s])
            re, im = trace_adjoint(*halves(first), *halves(second[s * N : (s + 1) * N]))
            out[2, s, t] = re
            out[3, s, t] = -im

    pairs(0)
    pairs(1)
    pairs(2)
    own.wait()
    arrived(0)

    @pl.when(c == 1)
    def _():
        edge_whole.start()

    fill(0)
    fill(1)
    trace_d(0)
    for s in range(S):
        dout[2 * s] = jnp.full((8, 128), dre[0, s], F32)
        dout[2 * s + 1] = jnp.full((8, 128), dim[0, s], F32)
    share = remote(dout, dnext, e_send.at[S + 1], e_recv.at[S + 1], before)
    share.start()
    box(0, right(0))
    trace_d(1)
    for copy in edges:
        copy.wait_recv()
    pairs(3)
    arrived(1)
    fill(2)
    fill(3)
    box(1, right(1))
    box(2, right(2))
    zlast[...] = right(3)
    trace_d(2)
    trace_d(3)
    arrived(2)

    @pl.when(c == 0)
    def _():
        edge_whole.wait_recv()

    box(3, zlast[...])
    share.wait_recv()
    for s in range(S):
        dre[T, s] = jnp.max(dnext[2 * s])
        dim[T, s] = jnp.max(dnext[2 * s + 1])
    for s in range(S):
        for t in range(T):
            ar, ai, br, bi = dre[t, s], dim[t, s], dre[t + 1, s], dim[t + 1, s]
            out[0, s, t] = ar * br + ai * bi
            out[1, s, t] = ai * br - ar * bi
    for g in range(3):
        all_sent(g)
    for copy in edges + [loc, share, hand(0, 0)]:
        copy.wait_send()

    @pl.when(c == 0)
    def _():
        edge_a.wait_send()

    @pl.when(c == 1)
    def _():
        edge_whole.wait_send()

    for i in range(1, NZ):
        for way in range(2):

            @pl.when(inside(way, i))
            def _():
                z_copy(way, i).wait_send()
                hand(way, i).wait_send()


def shards(perambulator, sink_elemental, source_elemental):
    dma = pltpu.SemaphoreType.DMA
    vmem = pltpu.VMEM
    return pl.pallas_call(
        kernel,
        out_shape=jax.ShapeDtypeStruct((4, S, T), F32),
        in_specs=[pl.BlockSpec(memory_space=pl.ANY)] * 3,
        out_specs=pl.BlockSpec(memory_space=pltpu.SMEM),
        scratch_shapes=[
            vmem((S, T + 1, N, W), BF),
            vmem((T + 1, W, W), BF),
            vmem((2, 16, ROWS, W), BF),
            vmem((S, W, W), BF),
            vmem((S, T, W, W), BF),
            vmem((T, S, N, W), F32),
            vmem((T, S, W, W), BF),
            vmem((S * N, W), F32),
            vmem((2 * S, 8, 128), F32),
            vmem((2 * S, 8, 128), F32),
            pltpu.SMEM((T + 1, S), F32),
            pltpu.SMEM((T + 1, S), F32),
            dma((T, S)),
            dma((2,)),
            dma((3, 2)),
            dma((3, 2)),
            dma((3,)),
            dma((3,)),
            dma((3, NYH, 2)),
            dma((3, NYH, 2)),
            dma((3, NYH)),
            dma((3, NYH)),
            dma,
            dma,
            dma((2, NZ - 1)),
            dma((2, NZ - 1)),
            dma((2, NZ)),
            dma((2, NZ)),
            dma((S + 3,)),
            dma((S + 3,)),
            pltpu.SemaphoreType.REGULAR,
        ],
        compiler_params=pltpu.CompilerParams(
            collective_id=0, has_side_effects=True, vmem_limit_bytes=60 * 1024 * 1024
        ),
        cost_estimate=pl.CostEstimate(flops=5_400_000_000, bytes_accessed=2_300_000, transcendentals=0),
    )(perambulator, sink_elemental, source_elemental.reshape(ROWS, W))


def solution(mesh):
    in_specs = (P("snk", "src", None, None), P("snk", "src", None), P("src", "snk", None))
    out_specs = P(None, "src", "snk")
    return jax.shard_map(shards, mesh=mesh, in_specs=in_specs, out_specs=out_specs, check_vma=False)
```

time: 117 us -> 40.8 us (0.35)
  the two profiles are of different devices: /device:TPU:4 before, /device:TPU:153 now
where the time goes in v2:
time: 40.8 us; the launch traced here: 40.5 us
  Pallas kernels  39.2 us (96%)
  local copies, waits for them, and re-layouts  1.28 us (3%)
    pallas_call x1, Pallas kernels, shards(): pl.pallas_call(kernel, out_shape=jax.ShapeDtypeStruct((4, S, T), F32), in...  39.2 us
    unnamed x1, local copies, waits for them, and re-layouts  1.28 us

profile of v2, /device:TPU:153, one launch (start us, length us, event | category | flops | bytes accessed | tf_op | source)
XLA Modules:
  0.0 40.5 jit_solution(3282862132853115049)
XLA Ops:
  0.0 39.2 %shard_map.37 = f32[4,2,4]{2,1,0:T(2,128)} custom-call(bf16[4,2,256,512]{3,2,1,0:T(8,128)(2,1)} %tau.1, bf16[4,16,512]{2,1,0:T(8,128)(2,1)} %sink.1, bf16[16,512]{1,0:T(8,128)(2,1)} %bitcast.1), custom_call_target="tpu_custom_call" | custom-call | flops 5400000000 | bytes 2300000 | tf_op jit(solution)/shard_map/pallas_call | solution.py:422
  39.2 1.3 %copy.5 = f32[4,2,4]{2,1,0:T(2,128)} copy(f32[4,2,4]{2,1,0:T(2,128)} %shard_map.37) | data formatting | bytes 256
